TPU v7x, 256 devices: a whole 4x4x8 slice. The times are simulated.
256 devices in a mesh: expert: 32 (over z, x), dp: 8 (over y, core).
Axes of the slice: x: 4, y: 4, z: 8, core: 2. Of those that a mesh axis runs over, the one named last changes fastest.
Arguments:
- tokens: bfloat16 [3072, 4096], P('expert', 'dp'), may hold values from -6 to 6
- route_weight: float32 [3072, 8], P('expert'), may hold values from 0.05 to 0.25
- route_expert: int32 [3072, 8], P('expert'), may hold values from 0 to 31, all different within a row; in each aligned block of 96 rows (0 to 95, 96 to 191, ...) at most 32 rows name the same one
- cotangent: bfloat16 [3072, 4096], P('expert', 'dp'), may hold values from -6 to 6
- gate_quant: bfloat16 [32, 4096, 1024], P('expert', None, 'dp'), may hold values from -0.09375 to 0.09375
- up_quant: bfloat16 [32, 4096, 1024], P('expert', None, 'dp'), may hold values from -0.09375 to 0.09375
- gate_scale: float32 [32, 32, 8], P('expert', None, 'dp'), may hold values from 0.5 to 2
- up_scale: float32 [32, 32, 8], P('expert', None, 'dp'), may hold values from 0.5 to 2
- down_quant: bfloat16 [32, 1024, 4096], P('expert', None, 'dp'), may hold values from -0.1875 to 0.1875
- down_scale: float32 [32, 8, 32], P('expert', None, 'dp'), may hold values from 0.5 to 2
- first_moment: float32 [32, 1024, 4096], P('expert', None, 'dp'), may hold values from -6 to 6
- second_moment: float32 [32, 1024, 4096], P('expert', None, 'dp'), may hold values from 0.5 to 8
- old_expert: int32 [32], replicated, may hold values from 0 to 31, each once
- new_holder: int32 [32], replicated, may hold values from 0 to 31, each once
Outputs:
- mixed: bfloat16 [3072, 4096], P('expert', 'dp')
- new_down: bfloat16 [32, 1024, 4096], P('expert', None, 'dp')
- new_first: float32 [32, 1024, 4096], P('expert', None, 'dp')
- new_second: float32 [32, 1024, 4096], P('expert', None, 'dp')
Inputs may be any that keep to these rules, and one draw needn't show every extreme that they name: `route_expert`: within each aligned block of 96 tokens (the tokens of one index of expert) no expert is named by more than 32 routes, a bound that some block reaches; a token names 8 different experts. `old_expert`: A permutation of the experts. `new_holder`: A permutation of the indices of expert.
All inputs are finite; a program needn't handle non-finite values.
Results may differ from a plain program's by a relative error of at most 0.0076.
Values may be sent and summed in bfloat16 or wider, within the bound.
A program may use at most 128 MiB of HBM per device.

v0:
```python
import jax
import jax.numpy as jnp
from jax import lax
from jax.sharding import PartitionSpec as P

QB = 128
beta_first = 0.9
beta_second = 0.95
adam_eps = 1e-08
learn_rate = 0.003
decay_rate = 0.1
step_count = 20


def dequantize(quant, scale):
    tiled = jnp.repeat(jnp.repeat(scale, QB, axis=0), QB, axis=1)
    return quant.astype(jnp.float32) * tiled


def adam_step(master, grad, first, second):
    first_new = beta_first * first + (1.0 - beta_first) * grad
    second_new = beta_second * second + (1.0 - beta_second) * grad * grad
    fix_first = 1.0 - beta_first**step_count
    fix_second = 1.0 - beta_second**step_count
    update = first_new / fix_first / (jnp.sqrt(second_new / fix_second) + adam_eps)
    fresh = (master - learn_rate * (update + decay_rate * master)).astype(jnp.bfloat16)
    return (fresh, first_new, second_new)


def holder_tables(old_expert, new_holder):
    number = old_expert.shape[0]
    labels = jnp.arange(number, dtype=jnp.int32)
    holds = (old_expert[:, None] == labels[None, :]).astype(jnp.int32)
    old_device = jnp.sum(holds * labels[:, None], axis=0)
    new_device = jnp.sum(holds * new_holder[:, None], axis=0)
    takes = (new_holder[:, None] == labels[None, :]).astype(jnp.int32)
    giver = jnp.sum(takes * labels[:, None], axis=0)
    return (old_device, new_device, giver)


def pack_rows(arrays, number):
    lines = []
    for array_item in arrays:
        line = array_item.reshape(-1)
        lines.append(line.reshape(number, -1))
    return jnp.concatenate(lines, axis=1)


def unpack_rows(packed, arrays):
    number = packed.shape[0]
    result = []
    offset = 0
    for array_item in arrays:
        span_cols = -(-array_item.size // number)
        block_rows = packed[:, offset : offset + span_cols]
        result.append(block_rows.reshape(-1).reshape(array_item.shape))
        offset = offset + span_cols
    return tuple(result)


def move_weights(arrays, giver):
    packed = pack_rows(arrays, giver.shape[0])
    spread = lax.all_to_all(packed, "expert", split_axis=0, concat_axis=0, tiled=True)
    settled = lax.all_to_all(
        jnp.take(spread, giver, axis=0), "expert", split_axis=0, concat_axis=0, tiled=True
    )
    return unpack_rows(settled, arrays)


def move_state(arrays, giver):
    packed = pack_rows(arrays, giver.shape[0])
    spread = lax.all_to_all(packed, "expert", split_axis=0, concat_axis=0, tiled=True)
    settled = lax.all_to_all(
        jnp.take(spread, giver, axis=0), "expert", split_axis=0, concat_axis=0, tiled=True
    )
    return unpack_rows(settled, arrays)


def plan_slots(route_expert, target_of, number, capacity):
    route_total = route_expert.shape[0] * route_expert.shape[1]
    flat_expert = route_expert.reshape(-1)
    labels = jnp.arange(number, dtype=jnp.int32)
    pick = (flat_expert[:, None] == labels[None, :]).astype(jnp.int32)
    target = jnp.sum(pick * target_of[None, :], axis=1)
    onehot = (target[:, None] == labels[None, :]).astype(jnp.int32)
    earlier = jnp.cumsum(onehot, axis=0) - onehot
    slot_index = jnp.sum(earlier * onehot, axis=1)
    route_place = target * capacity + slot_index
    slot_route = (
        jnp.full((number * capacity,), -1, jnp.int32)
        .at[route_place]
        .set(jnp.arange(route_total, dtype=jnp.int32))
    )
    return (route_place, slot_route)


def per_device(
    tokens,
    route_weight,
    route_expert,
    cotangent,
    gate_quant,
    up_quant,
    gate_scale,
    up_scale,
    down_quant,
    down_scale,
    first_moment,
    second_moment,
    old_expert,
    new_holder,
):
    number = lax.axis_size("expert")
    tok_rows, top_count = route_expert.shape
    model_width = gate_quant.shape[1]
    column_width = cotangent.shape[1]
    capacity = min(tok_rows, tok_rows * top_count // number * 4 // 3)
    old_device, new_device, giver = holder_tables(old_expert, new_holder)
    gate_quant, up_quant, down_quant = move_weights((gate_quant, up_quant, down_quant), giver)
    gate_scale, up_scale, down_scale, first_moment, second_moment = move_state(
        (gate_scale, up_scale, down_scale, first_moment, second_moment), giver
    )
    route_place, slot_route = plan_slots(route_expert, new_device, number, capacity)
    live_rows = slot_route >= 0
    safe_route = jnp.maximum(slot_route, 0)
    token_ids = safe_route // top_count
    weight_rows = jnp.where(
        live_rows, jnp.take(route_weight.reshape(-1), safe_route), jnp.float32(0.0)
    )
    back_rows = (
        weight_rows[:, None] * jnp.take(cotangent, token_ids, axis=0).astype(jnp.float32)
    ).astype(jnp.bfloat16)
    back_send = back_rows.reshape(number, capacity, column_width)
    whole_tokens = lax.all_gather(tokens, "dp", axis=1, tiled=True)
    sent_rows = jnp.take(whole_tokens, token_ids, axis=0).reshape(number, capacity, model_width)
    arrived, back_in = (
        lax.all_to_all(sent_rows, "expert", split_axis=0, concat_axis=0, tiled=True),
        lax.all_to_all(back_send, "expert", split_axis=0, concat_axis=0, tiled=True),
    )
    rows_in = arrived.reshape(-1, model_width)
    back_in = back_in.reshape(-1, column_width)
    gate_w = dequantize(gate_quant[0], gate_scale[0]).astype(jnp.bfloat16)
    up_w = dequantize(up_quant[0], up_scale[0]).astype(jnp.bfloat16)
    master = dequantize(down_quant[0], down_scale[0])
    down_w = master.astype(jnp.bfloat16)
    gate_val = jnp.dot(rows_in, gate_w, preferred_element_type=jnp.float32)
    up_val = jnp.dot(rows_in, up_w, preferred_element_type=jnp.float32)
    hidden_part = (jax.nn.silu(gate_val) * up_val).astype(jnp.bfloat16)
    hidden_full = lax.all_gather(hidden_part, "dp", axis=1, tiled=True)
    out_total = jnp.dot(hidden_full, down_w, preferred_element_type=jnp.float32)
    grad_total = lax.dot_general(
        hidden_full, back_in, (((0,), (0,)), ((), ())), preferred_element_type=jnp.float32
    )
    out_rows = out_total.astype(jnp.bfloat16).reshape(number, capacity, column_width)
    returned = lax.all_to_all(out_rows, "expert", split_axis=0, concat_axis=0, tiled=True).reshape(
        -1, column_width
    )
    picked = (
        jnp.take(returned, route_place, axis=0)
        .reshape(tok_rows, top_count, column_width)
        .astype(jnp.float32)
    )
    mixed = jnp.sum(picked * route_weight[:, :, None], axis=1).astype(jnp.bfloat16)
    fresh, first_new, second_new = adam_step(master, grad_total, first_moment[0], second_moment[0])
    fresh = fresh[None]
    first_new = first_new[None]
    second_new = second_new[None]
    return (mixed, fresh, first_new, second_new)


def solution(mesh):
    in_specs = (
        P("expert", "dp"),
        P("expert", None),
        P("expert", None),
        P("expert", "dp"),
        P("expert", None, "dp"),
        P("expert", None, "dp"),
        P("expert", None, "dp"),
        P("expert", None, "dp"),
        P("expert", None, "dp"),
        P("expert", None, "dp"),
        P("expert", None, "dp"),
        P("expert", None, "dp"),
        P(),
        P(),
    )
    out_specs = (
        P("expert", "dp"),
        P("expert", None, "dp"),
        P("expert", None, "dp"),
        P("expert", None, "dp"),
    )
    return jax.shard_map(
        per_device, mesh=mesh, in_specs=in_specs, out_specs=out_specs, check_vma=False
    )
```

profile of v0, /device:TPU:2, one launch (start us, length us, event | category | flops | bytes accessed | tf_op | source)
XLA Modules:
  0.0 698.2 jit_solution(656383670032208674)
XLA Ops:
  7.2 2.4 reshape_reshape.24
  9.7 1.3 reshape_reshape.25
  10.9 1.3 reshape_reshape.26
  12.2 2.0 maximum_bitcast_fusion
  14.7 3.8 reduce.10
  18.5 5.4 reshape.303
  23.9 11.8 %all-to-all-start.1 = ((bf16[32,2,24576]{2,1,0:T(2,128)(2,1)}), bf16[32,2,24576]{2,1,0:T(2,128)(2,1)S(1)}, u32[]{:S(2)}, u32[]{:S(2)}) async-start(bf16[32,2,24576]{2,1,0:T(2,128)(2,1)} %reshape.303), calls=%async_computation.1 | async-start | bytes 6291456 | tf_op jit(solution)/shard_map/all_to_all | solution.py:63
  36.0 2.7 reshape_reshape.30
  38.7 2.7 reshape_reshape.31
  41.5 1.3 dynamic-update-slice
  42.8 1.4 dynamic-update-slice.1
  44.2 1.4 dynamic-update-slice.2
  45.6 9.3 %dynamic-update-slice.3 = f32[32,32771]{1,0:T(8,128)} dynamic-update-slice(f32[32,32771]{1,0:T(8,128)} %dynamic-update-slice.2, f32[32,16384]{1,0:T(8,128)} %reshape_reshape.30, s32[]{} %constant.150, s32[]{} %constant.153) | dynamic-update-slice | bytes 4194308
  54.9 8.7 %dynamic-update-slice.4 = f32[32,32771]{1,0:T(8,128)} dynamic-update-slice(f32[32,32771]{1,0:T(8,128)} %dynamic-update-slice.3, f32[32,16384]{1,0:T(8,128)} %reshape_reshape.31, s32[]{} %constant.150, s32[]{} %constant.154) | dynamic-update-slice | bytes 4194308 | tf_op jit(solution)/shard_map/concatenate | solution.py:46
  63.5 9.8 %all_to_all.43 = f32[32,1,32771]{2,1,0:T(1,128)} reshape(f32[32,32771]{1,0:T(8,128)} %dynamic-update-slice.4) | data formatting | bytes 8389376 | tf_op jit(solution)/shard_map/all_to_all | solution.py:72
  73.5 33.4 %all-to-all-done.1 = bf16[32,2,24576]{2,1,0:T(2,128)(2,1)S(1)} async-done(((bf16[32,2,24576]{2,1,0:T(2,128)(2,1)}), bf16[32,2,24576]{2,1,0:T(2,128)(2,1)S(1)}, u32[]{:S(2)}, u32[]{:S(2)}) %all-to-all-start.1) | async-done | bytes 3145760 | tf_op jit(solution)/shard_map/all_to_all | solution.py:63
  106.9 7.8 %all-to-all-start.3 = ((f32[32,1,32771]{2,1,0:T(1,128)}), f32[32,1,32771]{2,1,0:T(1,128)}, u32[]{:S(2)}, u32[]{:S(2)}) async-start(f32[32,1,32771]{2,1,0:T(1,128)} %all_to_all.43), calls=%async_computation.3 | async-start | bytes 8421376 | tf_op jit(solution)/shard_map/all_to_all | solution.py:72
  114.7 12.4 %reshape.304 = bf16[32,1,49152]{2,1,0:T(2,128)(2,1)} reshape(bf16[32,2,24576]{2,1,0:T(2,128)(2,1)S(1)} %all-to-all-done.1) | data formatting | bytes 6291456
  127.2 6.2 copy.83
  133.4 4.3 gather_fusion.1
  137.7 2.3 bitcast_select_fusion.1
  139.9 3.7 reduce.11
  143.7 5.4 reshape.305
  149.1 59.0 %all-to-all-done.3 = f32[32,1,32771]{2,1,0:T(1,128)} async-done(((f32[32,1,32771]{2,1,0:T(1,128)}), f32[32,1,32771]{2,1,0:T(1,128)}, u32[]{:S(2)}, u32[]{:S(2)}) %all-to-all-start.3) | async-done | bytes 4194720 | tf_op jit(solution)/shard_map/all_to_all | solution.py:72
  208.1 8.3 %all-to-all-start.2 = ((bf16[32,2,24576]{2,1,0:T(2,128)(2,1)}), bf16[32,2,24576]{2,1,0:T(2,128)(2,1)}, u32[]{:S(2)}, u32[]{:S(2)}) async-start(bf16[32,2,24576]{2,1,0:T(2,128)(2,1)} %reshape.305), calls=%async_computation.2 | async-start | bytes 6291456 | tf_op jit(solution)/shard_map/all_to_all | solution.py:64
  216.5 4.4 copy.81
  220.9 7.6 %gather_fusion.2 = f32[32,32771]{1,0:T(8,128)} fusion(f32[32,32771]{1,0:T(8,128)} %bitcast.77, s32[1024]{0:T(1024)S(1)} %pad_clamp_fusion.1), kind=kCustom, calls=%fused_computation.2 | custom fusion | bytes 8389504 | tf_op jit(solution)/shard_map/jit(_take)/gather | solution.py:74
  228.5 2.5 bitcast_select_fusion
  231.0 6.3 copy.60
  237.3 50.3 %all-to-all-done.2 = bf16[32,2,24576]{2,1,0:T(2,128)(2,1)} async-done(((bf16[32,2,24576]{2,1,0:T(2,128)(2,1)}), bf16[32,2,24576]{2,1,0:T(2,128)(2,1)}, u32[]{:S(2)}, u32[]{:S(2)}) %all-to-all-start.2) | async-done | bytes 3145760 | tf_op jit(solution)/shard_map/all_to_all | solution.py:64
  287.6 7.4 %all-to-all-start.4 = ((f32[32,1,32771]{2,1,0:T(1,128)}), f32[32,1,32771]{2,1,0:T(1,128)}, u32[]{:S(2)}, u32[]{:S(2)}) async-start(f32[32,1,32771]{2,1,0:T(1,128)} %copy.60), calls=%async_computation.4 | async-start | bytes 8421376 | tf_op jit(solution)/shard_map/all_to_all | solution.py:73
  295.3 1.7 reduce-window.6
  297.5 3.4 scatter_custom_fusion
  301.0 14.1 %all_gather.6 = bf16[96,4096]{1,0:T(8,128)(2,1)S(1)} all-gather(bf16[96,512]{1,0:T(8,128)(2,1)S(1)} %copy-done.7), channel_id=1, replica_groups=mesh['expert'=32,'dp'=8] {'dp'}, dimensions={1}, use_global_device_ids=true | all-gather | bytes 884736 | tf_op jit(solution)/shard_map/all_gather | solution.py:134
  315.1 7.8 %gather_fusion = bf16[1024,4096]{1,0:T(8,128)(2,1)} fusion(bf16[96,4096]{1,0:T(8,128)(2,1)S(1)} %all_gather.6, s32[1024]{0:T(1024)S(1)} %get-tuple-element.17), kind=kCustom, calls=%fused_computation | custom fusion | bytes 16781312 | tf_op jit(solution)/shard_map/jit(_take)/gather | solution.py:135
  322.9 7.4 %broadcast_select_fusion = bf16[32,32,4096]{2,1,0:T(8,128)(2,1)} fusion(bf16[32,32,4096]{2,1,0:T(8,128)(2,1)} %bitcast.80, pred[32,32]{1,0:T(8,128)(4,1)S(1)} %broadcast_in_dim.103), kind=kLoop, calls=%fused_computation.7 | loop fusion | flops 4194304 | bytes 16778240 | tf_op jit(solution)/shard_map/jit(_take)/select_n | solution.py:135
  330.3 58.3 %all-to-all-done.4 = f32[32,1,32771]{2,1,0:T(1,128)} async-done(((f32[32,1,32771]{2,1,0:T(1,128)}), f32[32,1,32771]{2,1,0:T(1,128)}, u32[]{:S(2)}, u32[]{:S(2)}) %all-to-all-start.4) | async-done | bytes 4194720 | tf_op jit(solution)/shard_map/all_to_all | solution.py:73
  388.7 7.7 %all-to-all-start = ((bf16[32,32,4096]{2,1,0:T(8,128)(2,1)}), bf16[32,32,4096]{2,1,0:T(8,128)(2,1)}, u32[]{:S(2)}, u32[]{:S(2)}) async-start(bf16[32,32,4096]{2,1,0:T(8,128)(2,1)} %broadcast_select_fusion), calls=%async_computation | async-start | bytes 16777216 | tf_op jit(solution)/shard_map/all_to_all | solution.py:137
  396.6 4.5 gather_fusion.4
  401.2 4.0 gather_fusion.5
  405.2 1.3 multiply_convert_fusion
  406.5 18.9 %reshape.306 = bf16[32,1,49152]{2,1,0:T(2,128)(2,1)} reshape(bf16[32,2,24576]{2,1,0:T(2,128)(2,1)} %all-to-all-done.2) | data formatting | bytes 6291456
  425.4 6.2 copy.82
  431.7 2.5 copy.80
  434.4 2.2 multiply_convert_fusion.2
  436.7 2.3 convert_element_type.66
  439.1 2.3 convert_element_type.69
  441.4 145.2 %all-to-all-done = bf16[32,32,4096]{2,1,0:T(8,128)(2,1)} async-done(((bf16[32,32,4096]{2,1,0:T(8,128)(2,1)}), bf16[32,32,4096]{2,1,0:T(8,128)(2,1)}, u32[]{:S(2)}, u32[]{:S(2)}) %all-to-all-start) | async-done | bytes 8388640 | tf_op jit(solution)/shard_map/all_to_all | solution.py:137
  586.6 13.2 %all-to-all-start.6 = ((bf16[32,32,512]{2,1,0:T(8,128)(2,1)}), bf16[32,32,512]{2,1,0:T(8,128)(2,1)}, u32[]{:S(2)}, u32[]{:S(2)}) async-start(bf16[32,32,512]{2,1,0:T(8,128)(2,1)} %multiply_convert_fusion), calls=%async_computation.6 | async-start | bytes 2097152 | tf_op jit(solution)/shard_map/all_to_all | solution.py:138
  600.1 6.0 fusion.15
  606.1 6.4 fusion.1
  612.6 1.5 slice_convert_fusion
  614.0 1.7 reshape.234
  615.9 27.8 %all-gather.2.cloned.1.call-done = bf16[1024,1024]{1,0:T(8,128)(2,1)} async-done(((bf16[1024,128]{1,0:T(8,128)(2,1)}), bf16[1024,1024]{1,0:T(8,128)(2,1)}) %all-gather.2.cloned.1.call-update) | async-done | bytes 2097168 | tf_op jit(solution)/shard_map/all_gather | solution.py:149
  644.9 1.3 copy-done.2
  646.3 2.3 convolution_convert_fusion
  648.5 10.1 %all-to-all-start.5 = ((bf16[32,32,512]{2,1,0:T(8,128)(2,1)}), bf16[32,32,512]{2,1,0:T(8,128)(2,1)S(1)}, u32[]{:S(2)}, u32[]{:S(2)}) async-start(bf16[32,32,512]{2,1,0:T(8,128)(2,1)} %bitcast.12), calls=%async_computation.5 | async-start | bytes 2097152 | tf_op jit(solution)/shard_map/all_to_all | solution.py:155
  658.7 4.7 slice_multiply_fusion
  663.4 2.7 mul.139
  666.1 1.5 mul.146
  667.6 9.3 %fusion.5 = (f32[1,1024,512]{2,1,0:T(8,128)}, bf16[1,1024,512]{2,1,0:T(8,128)(2,1)}, f32[1,1024,512]{2,1,0:T(8,128)}) fusion(f32[1024,512]{1,0:T(8,128)} %mul.146, f32[1024,512]{1,0:T(8,128)} %mul.139, f32[1024,512]{1,0:T(8,128)} %copy-done.3, f32[128,8,4,128]{3,2,1,0:T(4,128)} %bitcast.87, bf16[1024,1024]{1,0:T(8,128)(2,1)} %all-gather.2.cloned.1.call-done, ...), kind=kOutput, calls=%fused_computation.34 | convolution fusion | flops 1081606144 | bytes 16777216 | tf_op jit(solution)/shard_map/dot_general | solution.py:151
  676.9 10.2 %all-to-all-done.5 = bf16[32,32,512]{2,1,0:T(8,128)(2,1)S(1)} async-done(((bf16[32,32,512]{2,1,0:T(8,128)(2,1)}), bf16[32,32,512]{2,1,0:T(8,128)(2,1)S(1)}, u32[]{:S(2)}, u32[]{:S(2)}) %all-to-all-start.5) | async-done | bytes 1048608 | tf_op jit(solution)/shard_map/all_to_all | solution.py:155
  687.2 2.7 gather_fusion.3
  689.8 1.3 multiply_reduce_fusion
  (68 shorter events, 4.3 us)
Async XLA Ops:
  7.2 394.1 %copy-start = (bf16[96,512]{1,0:T(8,128)(2,1)S(1)}, bf16[96,512]{1,0:T(8,128)(2,1)}, u32[]{:S(2)}) copy-start(bf16[96,512]{1,0:T(8,128)(2,1)} %param.17) | copy-start | bytes 294916
  7.2 2.5 copy-start.4
  7.2 3.7 copy-start.5
  23.9 11.8 %copy-start.11 = (f32[1,32,1]{1,2,0:T(1,128)S(1)}, f32[1,32,1]{1,2,0:T(1,128)}, u32[]{:S(2)}) copy-start(f32[1,32,1]{1,2,0:T(1,128)} %param.20) | copy-start | bytes 388
  23.9 11.9 %copy-start.12 = (f32[1,32,1]{1,2,0:T(1,128)S(1)}, f32[1,32,1]{1,2,0:T(1,128)}, u32[]{:S(2)}) copy-start(f32[1,32,1]{1,2,0:T(1,128)} %param.21) | copy-start | bytes 388
  23.9 12.0 %copy-start.10 = (f32[1,8,4]{1,2,0:T(4,128)S(1)}, f32[1,8,4]{1,2,0:T(4,128)}, u32[]{:S(2)}) copy-start(f32[1,8,4]{1,2,0:T(4,128)} %param.23) | copy-start | bytes 388
  23.9 83.0 %all-to-all-start.1 = ((bf16[32,2,24576]{2,1,0:T(2,128)(2,1)}), bf16[32,2,24576]{2,1,0:T(2,128)(2,1)S(1)}, u32[]{:S(2)}, u32[]{:S(2)}) async-start(bf16[32,2,24576]{2,1,0:T(2,128)(2,1)} %reshape.303), calls=%async_computation.1 | async-start | bytes 6291456 | tf_op jit(solution)/shard_map/all_to_all | solution.py:63
  63.5 9.8 %copy-start.13 = (s32[32]{0:T(128)S(1)}, s32[32]{0:T(128)}, u32[]{:S(2)}) copy-start(s32[32]{0:T(128)} %param.27) | copy-start | bytes 388
  63.5 9.8 %copy-start.14 = (s32[32]{0:T(128)S(1)}, s32[32]{0:T(128)}, u32[]{:S(2)}) copy-start(s32[32]{0:T(128)} %param.26) | copy-start | bytes 388
  106.9 101.2 %all-to-all-start.3 = ((f32[32,1,32771]{2,1,0:T(1,128)}), f32[32,1,32771]{2,1,0:T(1,128)}, u32[]{:S(2)}, u32[]{:S(2)}) async-start(f32[32,1,32771]{2,1,0:T(1,128)} %all_to_all.43), calls=%async_computation.3 | async-start | bytes 8421376 | tf_op jit(solution)/shard_map/all_to_all | solution.py:72
  208.1 79.5 %all-to-all-start.2 = ((bf16[32,2,24576]{2,1,0:T(2,128)(2,1)}), bf16[32,2,24576]{2,1,0:T(2,128)(2,1)}, u32[]{:S(2)}, u32[]{:S(2)}) async-start(bf16[32,2,24576]{2,1,0:T(2,128)(2,1)} %reshape.305), calls=%async_computation.2 | async-start | bytes 6291456 | tf_op jit(solution)/shard_map/all_to_all | solution.py:64
  237.3 57.7 %copy-start.8 = (s32[96,8]{0,1:T(8,128)S(1)}, s32[96,8]{0,1:T(8,128)}, u32[]{:S(2)}) copy-start(s32[96,8]{0,1:T(8,128)} %param.16) | copy-start | bytes 9220
  237.3 63.7 %copy-start.7 = (bf16[96,512]{1,0:T(8,128)(2,1)S(1)}, bf16[96,512]{1,0:T(8,128)(2,1)}, u32[]{:S(2)}) copy-start(bf16[96,512]{1,0:T(8,128)(2,1)} %param.14) | copy-start | bytes 294916
  287.6 101.0 %all-to-all-start.4 = ((f32[32,1,32771]{2,1,0:T(1,128)}), f32[32,1,32771]{2,1,0:T(1,128)}, u32[]{:S(2)}, u32[]{:S(2)}) async-start(f32[32,1,32771]{2,1,0:T(1,128)} %copy.60), calls=%async_computation.4 | async-start | bytes 8421376 | tf_op jit(solution)/shard_map/all_to_all | solution.py:73
  330.3 66.1 %copy-start.9 = (f32[96,8]{0,1:T(8,128)S(1)}, f32[96,8]{0,1:T(8,128)}, u32[]{:S(2)}) copy-start(f32[96,8]{0,1:T(8,128)} %param.15) | copy-start | bytes 9220
  388.7 198.0 %all-to-all-start = ((bf16[32,32,4096]{2,1,0:T(8,128)(2,1)}), bf16[32,32,4096]{2,1,0:T(8,128)(2,1)}, u32[]{:S(2)}, u32[]{:S(2)}) async-start(bf16[32,32,4096]{2,1,0:T(8,128)(2,1)} %broadcast_select_fusion), calls=%async_computation | async-start | bytes 16777216 | tf_op jit(solution)/shard_map/all_to_all | solution.py:137
  434.1 2.6 copy-start.1
  586.6 61.9 %all-to-all-start.6 = ((bf16[32,32,512]{2,1,0:T(8,128)(2,1)}), bf16[32,32,512]{2,1,0:T(8,128)(2,1)}, u32[]{:S(2)}, u32[]{:S(2)}) async-start(bf16[32,32,512]{2,1,0:T(8,128)(2,1)} %multiply_convert_fusion), calls=%async_computation.6 | async-start | bytes 2097152 | tf_op jit(solution)/shard_map/all_to_all | solution.py:138
  599.8 43.9 %all-gather.2.cloned.1.call-start = ((), (), s32[]{:S(2)}) async-start(), calls=%async_computation.7 | async-start | bytes 2359296 | tf_op jit(solution)/shard_map/all_gather | solution.py:149
  600.1 6.0 copy-start.6
  615.8 32.8 %copy-start.3 = (f32[1024,512]{1,0:T(8,128)}, f32[1024,512]{1,0:T(8,128)S(1)}, u32[]{:S(2)}) copy-start(f32[1024,512]{1,0:T(8,128)S(1)} %reshape.234) | copy-start | bytes 6291460
  643.6 2.6 copy-start.15
  644.9 1.3 copy-start.2
  648.5 38.6 %all-to-all-start.5 = ((bf16[32,32,512]{2,1,0:T(8,128)(2,1)}), bf16[32,32,512]{2,1,0:T(8,128)(2,1)S(1)}, u32[]{:S(2)}, u32[]{:S(2)}) async-start(bf16[32,32,512]{2,1,0:T(8,128)(2,1)} %bitcast.12), calls=%async_computation.5 | async-start | bytes 2097152 | tf_op jit(solution)/shard_map/all_to_all | solution.py:155
Sparse Core Ops, SparseCore 0:
  612.7 30.9 all-gather.1
where the time goes:
time: 706 us; the launch traced here: 698 us
  waiting for transfers between devices  384 us (54%)
  local copies, waits for them, and re-layouts  160 us (23%)
  starting transfers between devices  66.5 us (9%)
  other arithmetic  34.7 us (5%)
  matrix products  24 us (3%)
  between operations  14.6 us (2%)
  blocking collectives  14.1 us (2%)
    all_to_all x1, waiting for transfers between devices, per_device(): lax.all_to_all(sent_rows, 'expert', split_axis=0, concat_axis=0, tiled=True)  145 us
    unnamed x47, local copies, waits for them, and re-layouts  76.8 us
    all_to_all x1, waiting for transfers between devices, move_state(): lax.all_to_all(packed, 'expert', split_axis=0, concat_axis=0, tiled=True)  59 us
    all_to_all x1, waiting for transfers between devices, move_state(): lax.all_to_all(jnp.take(spread, giver, axis=0), 'expert', split_axis=0, c...  58.3 us
    all_to_all x1, waiting for transfers between devices, move_weights(): lax.all_to_all(jnp.take(spread, giver, axis=0), 'expert', split_axis=0, c...  50.3 us
    all_to_all x1, waiting for transfers between devices, move_weights(): lax.all_to_all(packed, 'expert', split_axis=0, concat_axis=0, tiled=True)  33.4 us
    all_gather x1, waiting for transfers between devices, per_device(): hidden_full = lax.all_gather(hidden_part, 'dp', axis=1, tiled=True)  27.8 us
  transfers between devices with their start and end apart: 8, of which 7 were waited for; matrix products, arithmetic and copies ran while one was open for 27% of the time, Pallas kernels for 0%

commit v1 on v0

--- a/solution.py
+++ b/solution.py
@@ -2,6 +2,7 @@
 import jax.numpy as jnp
 from jax import lax
 from jax.sharding import PartitionSpec as P
+from jax.lax import axis_index, axis_size, ppermute
 
 QB = 128
 beta_first = 0.9
@@ -10,6 +11,20 @@
 learn_rate = 0.003
 decay_rate = 0.1
 step_count = 20
+
+
+def _watch_side(inner_x, device_axis):
+    axis_n = axis_size(device_axis)
+    found_now = range(axis_n)
+    main = map(lambda idx: (idx, (idx + 1) % axis_n), found_now)
+    rows = list(main)
+    known = [None] * axis_n
+    known[axis_n - 1] = inner_x
+    for k in range(axis_n - 2, -1, -1):
+        known[k] = ppermute(known[k + 1], device_axis, rows)
+    far_arr = jnp.concatenate(known, axis=1)
+    local_out = (axis_index(device_axis) + 1) * inner_x.shape[1]
+    return jnp.roll(far_arr, shift=local_out, axis=1)
 
 
 def dequantize(quant, scale):
@@ -131,7 +146,7 @@
         weight_rows[:, None] * jnp.take(cotangent, token_ids, axis=0).astype(jnp.float32)
     ).astype(jnp.bfloat16)
     back_send = back_rows.reshape(number, capacity, column_width)
-    whole_tokens = lax.all_gather(tokens, "dp", axis=1, tiled=True)
+    whole_tokens = _watch_side(tokens, "dp")
     sent_rows = jnp.take(whole_tokens, token_ids, axis=0).reshape(number, capacity, model_width)
     arrived, back_in = (
         lax.all_to_all(sent_rows, "expert", split_axis=0, concat_axis=0, tiled=True),

time: 706 us -> 706 us (level)
  blocking collectives: 14.1 us -> 0 us
  waiting for transfers between devices: 384 us -> 398 us
    ppermute x0 -> x7, waiting for transfers between devices: none -> 30.6 us  [_watch_side(): known[k] = ppermute(known[k + 1], device_axis, rows)]
    all_to_all x1, waiting for transfers between devices: 58.3 us -> 41.3 us  [move_state(): lax.all_to_all(jnp.take(spread, giver, axis=0), 'expert', split_axis=0, c...]
    all_gather x1 -> x0, blocking collectives: 14.1 us -> none  [per_device(): whole_tokens = lax.all_gather(tokens, 'dp', axis=1, tiled=True)]
    unnamed x47 -> x62, local copies, waits for them, and re-layouts: 76.8 us -> 77 us
  transfers between devices with their start and end apart: 8 -> 15, of which waited for: 7 -> 14; matrix products, arithmetic and copies ran while one was open for 27% -> 27% of each run, Pallas kernels for 0% -> 0%
where the time goes in v1:
time: 706 us; the launch traced here: 698 us
  waiting for transfers between devices  398 us (56%)
  local copies, waits for them, and re-layouts  160 us (23%)
  starting transfers between devices  66.5 us (9%)
  other arithmetic  34.7 us (5%)
  matrix products  24.1 us (3%)
  between operations  14.8 us (2%)
    all_to_all x1, waiting for transfers between devices, per_device(): lax.all_to_all(sent_rows, 'expert', split_axis=0, concat_axis=0, tiled=True)  145 us
    unnamed x62, local copies, waits for them, and re-layouts  77 us
    all_to_all x1, waiting for transfers between devices, move_state(): lax.all_to_all(packed, 'expert', split_axis=0, concat_axis=0, tiled=True)  59 us
    all_to_all x1, waiting for transfers between devices, move_weights(): lax.all_to_all(jnp.take(spread, giver, axis=0), 'expert', split_axis=0, c...  50.3 us
    all_to_all x1, waiting for transfers between devices, move_state(): lax.all_to_all(jnp.take(spread, giver, axis=0), 'expert', split_axis=0, c...  41.3 us
    all_to_all x1, waiting for transfers between devices, move_weights(): lax.all_to_all(packed, 'expert', split_axis=0, concat_axis=0, tiled=True)  33.4 us
    ppermute x7, waiting for transfers between devices, _watch_side(): known[k] = ppermute(known[k + 1], device_axis, rows)  30.6 us
    all_gather x1, waiting for transfers between devices, per_device(): hidden_full = lax.all_gather(hidden_part, 'dp', axis=1, tiled=True)  27.8 us
  transfers between devices with their start and end apart: 15, of which 14 were waited for; matrix products, arithmetic and copies ran while one was open for 27% of the time, Pallas kernels for 0%

profile of v1, /device:TPU:2, one launch (start us, length us, event | category | flops | bytes accessed | tf_op | source)
XLA Modules:
  0.0 698.2 jit_solution(5718206393414813421)
XLA Ops:
  7.2 2.4 reshape_reshape.24
  12.2 2.0 maximum_bitcast_fusion
  14.7 3.8 reduce.10
  18.4 5.4 reshape.303
  23.9 11.8 %all-to-all-start.1 = ((bf16[32,2,24576]{2,1,0:T(2,128)(2,1)}), bf16[32,2,24576]{2,1,0:T(2,128)(2,1)S(1)}, u32[]{:S(2)}, u32[]{:S(2)}) async-start(bf16[32,2,24576]{2,1,0:T(2,128)(2,1)} %reshape.303), calls=%async_computation.1 | async-start | bytes 6291456 | tf_op jit(solution)/shard_map/all_to_all | solution.py:78
  36.0 2.7 reshape_reshape.30
  38.7 2.7 reshape_reshape.31
  42.8 1.4 dynamic-update-slice.1
  44.2 1.4 dynamic-update-slice.2
  45.6 9.3 %dynamic-update-slice.3 = f32[32,32771]{1,0:T(8,128)} dynamic-update-slice(f32[32,32771]{1,0:T(8,128)} %dynamic-update-slice.2, f32[32,16384]{1,0:T(8,128)} %reshape_reshape.30, s32[]{} %constant.178, s32[]{} %constant.181) | dynamic-update-slice | bytes 4194308
  54.9 8.6 %dynamic-update-slice.4 = f32[32,32771]{1,0:T(8,128)} dynamic-update-slice(f32[32,32771]{1,0:T(8,128)} %dynamic-update-slice.3, f32[32,16384]{1,0:T(8,128)} %reshape_reshape.31, s32[]{} %constant.178, s32[]{} %constant.182) | dynamic-update-slice | bytes 4194308 | tf_op jit(solution)/shard_map/concatenate | solution.py:61
  63.5 9.8 %all_to_all.43 = f32[32,1,32771]{2,1,0:T(1,128)} reshape(f32[32,32771]{1,0:T(8,128)} %dynamic-update-slice.4) | data formatting | bytes 8389376 | tf_op jit(solution)/shard_map/all_to_all | solution.py:87
  73.5 33.4 %all-to-all-done.1 = bf16[32,2,24576]{2,1,0:T(2,128)(2,1)S(1)} async-done(((bf16[32,2,24576]{2,1,0:T(2,128)(2,1)}), bf16[32,2,24576]{2,1,0:T(2,128)(2,1)S(1)}, u32[]{:S(2)}, u32[]{:S(2)}) %all-to-all-start.1) | async-done | bytes 3145760 | tf_op jit(solution)/shard_map/all_to_all | solution.py:78
  106.9 7.8 %all-to-all-start.3 = ((f32[32,1,32771]{2,1,0:T(1,128)}), f32[32,1,32771]{2,1,0:T(1,128)}, u32[]{:S(2)}, u32[]{:S(2)}) async-start(f32[32,1,32771]{2,1,0:T(1,128)} %all_to_all.43), calls=%async_computation.3 | async-start | bytes 8421376 | tf_op jit(solution)/shard_map/all_to_all | solution.py:87
  114.7 12.5 %reshape.304 = bf16[32,1,49152]{2,1,0:T(2,128)(2,1)} reshape(bf16[32,2,24576]{2,1,0:T(2,128)(2,1)S(1)} %all-to-all-done.1) | data formatting | bytes 6291456
  127.2 6.2 copy.83
  133.5 4.3 gather_fusion.1
  137.8 2.3 bitcast_select_fusion.1
  140.0 3.7 reduce.11
  143.8 5.4 reshape.305
  149.2 59.0 %all-to-all-done.3 = f32[32,1,32771]{2,1,0:T(1,128)} async-done(((f32[32,1,32771]{2,1,0:T(1,128)}), f32[32,1,32771]{2,1,0:T(1,128)}, u32[]{:S(2)}, u32[]{:S(2)}) %all-to-all-start.3) | async-done | bytes 4194720 | tf_op jit(solution)/shard_map/all_to_all | solution.py:87
  208.1 8.3 %all-to-all-start.2 = ((bf16[32,2,24576]{2,1,0:T(2,128)(2,1)}), bf16[32,2,24576]{2,1,0:T(2,128)(2,1)}, u32[]{:S(2)}, u32[]{:S(2)}) async-start(bf16[32,2,24576]{2,1,0:T(2,128)(2,1)} %reshape.305), calls=%async_computation.2 | async-start | bytes 6291456 | tf_op jit(solution)/shard_map/all_to_all | solution.py:79
  216.5 4.4 copy.81
  220.9 7.6 %gather_fusion.2 = f32[32,32771]{1,0:T(8,128)} fusion(f32[32,32771]{1,0:T(8,128)} %bitcast.77, s32[1024]{0:T(1024)S(1)} %pad_clamp_fusion.1), kind=kCustom, calls=%fused_computation.2 | custom fusion | bytes 8389504 | tf_op jit(solution)/shard_map/jit(_take)/gather | solution.py:89
  228.5 2.5 bitcast_select_fusion
  231.1 6.3 copy.60
  237.3 50.3 %all-to-all-done.2 = bf16[32,2,24576]{2,1,0:T(2,128)(2,1)} async-done(((bf16[32,2,24576]{2,1,0:T(2,128)(2,1)}), bf16[32,2,24576]{2,1,0:T(2,128)(2,1)}, u32[]{:S(2)}, u32[]{:S(2)}) %all-to-all-start.2) | async-done | bytes 3145760 | tf_op jit(solution)/shard_map/all_to_all | solution.py:79
  287.6 7.4 %all-to-all-start.4 = ((f32[32,1,32771]{2,1,0:T(1,128)}), f32[32,1,32771]{2,1,0:T(1,128)}, u32[]{:S(2)}, u32[]{:S(2)}) async-start(f32[32,1,32771]{2,1,0:T(1,128)} %copy.60), calls=%async_computation.4 | async-start | bytes 8421376 | tf_op jit(solution)/shard_map/all_to_all | solution.py:88
  295.3 5.0 collective-permute-done
  300.3 1.7 reduce-window.6
  302.0 3.5 collective-permute-done.1
  305.8 5.0 collective-permute-done.2
  310.9 5.1 collective-permute-done.3
  316.1 3.6 scatter_custom_fusion
  319.6 1.7 collective-permute-done.4
  321.3 5.2 collective-permute-done.5
  326.7 5.1 collective-permute-done.6
  332.1 7.8 %gather_fusion = bf16[1024,4096]{1,0:T(8,128)(2,1)} fusion(bf16[96,4096]{1,0:T(8,128)(2,1)S(1)} %constant_dynamic-slice_fusion, s32[1024]{0:T(1024)S(1)} %get-tuple-element.17), kind=kCustom, calls=%fused_computation | custom fusion | bytes 16781312 | tf_op jit(solution)/shard_map/jit(_take)/gather | solution.py:150
  339.9 7.4 %broadcast_select_fusion = bf16[32,32,4096]{2,1,0:T(8,128)(2,1)} fusion(bf16[32,32,4096]{2,1,0:T(8,128)(2,1)} %bitcast.80, pred[32,32]{1,0:T(8,128)(4,1)S(1)} %broadcast_in_dim.103), kind=kLoop, calls=%fused_computation.7 | loop fusion | flops 4194304 | bytes 16778240 | tf_op jit(solution)/shard_map/jit(_take)/select_n | solution.py:150
  347.3 41.3 %all-to-all-done.4 = f32[32,1,32771]{2,1,0:T(1,128)} async-done(((f32[32,1,32771]{2,1,0:T(1,128)}), f32[32,1,32771]{2,1,0:T(1,128)}, u32[]{:S(2)}, u32[]{:S(2)}) %all-to-all-start.4) | async-done | bytes 4194720 | tf_op jit(solution)/shard_map/all_to_all | solution.py:88
  388.7 7.6 %all-to-all-start = ((bf16[32,32,4096]{2,1,0:T(8,128)(2,1)}), bf16[32,32,4096]{2,1,0:T(8,128)(2,1)}, u32[]{:S(2)}, u32[]{:S(2)}) async-start(bf16[32,32,4096]{2,1,0:T(8,128)(2,1)} %broadcast_select_fusion), calls=%async_computation | async-start | bytes 16777216 | tf_op jit(solution)/shard_map/all_to_all | solution.py:152
  396.6 4.5 gather_fusion.4
  401.2 4.0 gather_fusion.5
  406.6 18.9 %reshape.306 = bf16[32,1,49152]{2,1,0:T(2,128)(2,1)} reshape(bf16[32,2,24576]{2,1,0:T(2,128)(2,1)} %all-to-all-done.2) | data formatting | bytes 6291456
  425.5 6.2 copy.82
  431.7 2.5 copy.80
  434.4 2.1 multiply_convert_fusion.2
  436.8 2.3 convert_element_type.66
  439.1 2.3 convert_element_type.69
  441.5 145.2 %all-to-all-done = bf16[32,32,4096]{2,1,0:T(8,128)(2,1)} async-done(((bf16[32,32,4096]{2,1,0:T(8,128)(2,1)}), bf16[32,32,4096]{2,1,0:T(8,128)(2,1)}, u32[]{:S(2)}, u32[]{:S(2)}) %all-to-all-start) | async-done | bytes 8388640 | tf_op jit(solution)/shard_map/all_to_all | solution.py:152
  586.6 13.2 %all-to-all-start.6 = ((bf16[32,32,512]{2,1,0:T(8,128)(2,1)}), bf16[32,32,512]{2,1,0:T(8,128)(2,1)}, u32[]{:S(2)}, u32[]{:S(2)}) async-start(bf16[32,32,512]{2,1,0:T(8,128)(2,1)} %multiply_convert_fusion), calls=%async_computation.6 | async-start | bytes 2097152 | tf_op jit(solution)/shard_map/all_to_all | solution.py:153
  600.1 6.0 fusion.15
  606.1 6.4 fusion.1
  612.6 1.5 slice_convert_fusion
  614.0 1.7 reshape.234
  615.9 27.8 %all-gather.2.cloned.1.call-done = bf16[1024,1024]{1,0:T(8,128)(2,1)} async-done(((bf16[1024,128]{1,0:T(8,128)(2,1)}), bf16[1024,1024]{1,0:T(8,128)(2,1)}) %all-gather.2.cloned.1.call-update) | async-done | bytes 2097168 | tf_op jit(solution)/shard_map/all_gather | solution.py:164
  646.3 2.3 convolution_convert_fusion
  648.5 10.1 %all-to-all-start.5 = ((bf16[32,32,512]{2,1,0:T(8,128)(2,1)}), bf16[32,32,512]{2,1,0:T(8,128)(2,1)S(1)}, u32[]{:S(2)}, u32[]{:S(2)}) async-start(bf16[32,32,512]{2,1,0:T(8,128)(2,1)} %bitcast.12), calls=%async_computation.5 | async-start | bytes 2097152 | tf_op jit(solution)/shard_map/all_to_all | solution.py:170
  658.7 4.7 slice_multiply_fusion
  663.4 2.7 mul.143
  666.1 1.5 mul.150
  667.6 9.3 %fusion.5 = (f32[1,1024,512]{2,1,0:T(8,128)}, bf16[1,1024,512]{2,1,0:T(8,128)(2,1)}, f32[1,1024,512]{2,1,0:T(8,128)}) fusion(f32[1024,512]{1,0:T(8,128)} %mul.150, f32[1024,512]{1,0:T(8,128)} %mul.143, f32[1024,512]{1,0:T(8,128)} %copy-done.3, f32[128,8,4,128]{3,2,1,0:T(4,128)} %bitcast.87, bf16[1024,1024]{1,0:T(8,128)(2,1)} %all-gather.2.cloned.1.call-done, ...), kind=kOutput, calls=%fused_computation.34 | convolution fusion | flops 1081606144 | bytes 16777216 | tf_op jit(solution)/shard_map/dot_general | solution.py:166
  677.0 10.2 %all-to-all-done.5 = bf16[32,32,512]{2,1,0:T(8,128)(2,1)S(1)} async-done(((bf16[32,32,512]{2,1,0:T(8,128)(2,1)}), bf16[32,32,512]{2,1,0:T(8,128)(2,1)S(1)}, u32[]{:S(2)}, u32[]{:S(2)}) %all-to-all-start.5) | async-done | bytes 1048608 | tf_op jit(solution)/shard_map/all_to_all | solution.py:170
  687.2 2.7 gather_fusion.3
  (98 shorter events, 12.3 us)
Async XLA Ops:
  7.2 394.1 %copy-start = (bf16[96,512]{1,0:T(8,128)(2,1)S(1)}, bf16[96,512]{1,0:T(8,128)(2,1)}, u32[]{:S(2)}) copy-start(bf16[96,512]{1,0:T(8,128)(2,1)} %param.17) | copy-start | bytes 294916
  7.2 2.5 copy-start.4
  7.2 3.7 copy-start.5
  23.9 11.8 %copy-start.11 = (f32[1,32,1]{1,2,0:T(1,128)S(1)}, f32[1,32,1]{1,2,0:T(1,128)}, u32[]{:S(2)}) copy-start(f32[1,32,1]{1,2,0:T(1,128)} %param.20) | copy-start | bytes 388
  23.9 11.9 %copy-start.12 = (f32[1,32,1]{1,2,0:T(1,128)S(1)}, f32[1,32,1]{1,2,0:T(1,128)}, u32[]{:S(2)}) copy-start(f32[1,32,1]{1,2,0:T(1,128)} %param.21) | copy-start | bytes 388
  23.9 12.0 %copy-start.10 = (f32[1,8,4]{1,2,0:T(4,128)S(1)}, f32[1,8,4]{1,2,0:T(4,128)}, u32[]{:S(2)}) copy-start(f32[1,8,4]{1,2,0:T(4,128)} %param.23) | copy-start | bytes 388
  23.9 83.0 %all-to-all-start.1 = ((bf16[32,2,24576]{2,1,0:T(2,128)(2,1)}), bf16[32,2,24576]{2,1,0:T(2,128)(2,1)S(1)}, u32[]{:S(2)}, u32[]{:S(2)}) async-start(bf16[32,2,24576]{2,1,0:T(2,128)(2,1)} %reshape.303), calls=%async_computation.1 | async-start | bytes 6291456 | tf_op jit(solution)/shard_map/all_to_all | solution.py:78
  63.5 9.8 %copy-start.13 = (s32[32]{0:T(128)S(1)}, s32[32]{0:T(128)}, u32[]{:S(2)}) copy-start(s32[32]{0:T(128)} %param.27) | copy-start | bytes 388
  63.5 9.8 %copy-start.14 = (s32[32]{0:T(128)S(1)}, s32[32]{0:T(128)}, u32[]{:S(2)}) copy-start(s32[32]{0:T(128)} %param.26) | copy-start | bytes 388
  106.9 101.2 %all-to-all-start.3 = ((f32[32,1,32771]{2,1,0:T(1,128)}), f32[32,1,32771]{2,1,0:T(1,128)}, u32[]{:S(2)}, u32[]{:S(2)}) async-start(f32[32,1,32771]{2,1,0:T(1,128)} %all_to_all.43), calls=%async_computation.3 | async-start | bytes 8421376 | tf_op jit(solution)/shard_map/all_to_all | solution.py:87
  208.1 79.5 %all-to-all-start.2 = ((bf16[32,2,24576]{2,1,0:T(2,128)(2,1)}), bf16[32,2,24576]{2,1,0:T(2,128)(2,1)}, u32[]{:S(2)}, u32[]{:S(2)}) async-start(bf16[32,2,24576]{2,1,0:T(2,128)(2,1)} %reshape.305), calls=%async_computation.2 | async-start | bytes 6291456 | tf_op jit(solution)/shard_map/all_to_all | solution.py:79
  237.3 57.7 %copy-start.7 = (bf16[96,512]{1,0:T(8,128)(2,1)S(1)}, bf16[96,512]{1,0:T(8,128)(2,1)}, u32[]{:S(2)}) copy-start(bf16[96,512]{1,0:T(8,128)(2,1)} %param.14) | copy-start | bytes 294916
  237.3 57.7 %copy-start.8 = (s32[96,8]{0,1:T(8,128)S(1)}, s32[96,8]{0,1:T(8,128)}, u32[]{:S(2)}) copy-start(s32[96,8]{0,1:T(8,128)} %param.16) | copy-start | bytes 9220
  287.6 101.0 %all-to-all-start.4 = ((f32[32,1,32771]{2,1,0:T(1,128)}), f32[32,1,32771]{2,1,0:T(1,128)}, u32[]{:S(2)}, u32[]{:S(2)}) async-start(f32[32,1,32771]{2,1,0:T(1,128)} %copy.60), calls=%async_computation.4 | async-start | bytes 8421376 | tf_op jit(solution)/shard_map/all_to_all | solution.py:88
  295.0 5.3 collective-permute-start
  300.3 5.3 collective-permute-start.1
  305.5 5.3 collective-permute-start.2
  310.8 5.3 collective-permute-start.3
  316.0 5.3 collective-permute-start.4
  321.3 5.3 collective-permute-start.5
  326.6 5.3 collective-permute-start.6
  347.3 49.1 %copy-start.9 = (f32[96,8]{0,1:T(8,128)S(1)}, f32[96,8]{0,1:T(8,128)}, u32[]{:S(2)}) copy-start(f32[96,8]{0,1:T(8,128)} %param.15) | copy-start | bytes 9220
  388.7 198.0 %all-to-all-start = ((bf16[32,32,4096]{2,1,0:T(8,128)(2,1)}), bf16[32,32,4096]{2,1,0:T(8,128)(2,1)}, u32[]{:S(2)}, u32[]{:S(2)}) async-start(bf16[32,32,4096]{2,1,0:T(8,128)(2,1)} %broadcast_select_fusion), calls=%async_computation | async-start | bytes 16777216 | tf_op jit(solution)/shard_map/all_to_all | solution.py:152
  434.2 2.6 copy-start.1
  586.6 61.9 %all-to-all-start.6 = ((bf16[32,32,512]{2,1,0:T(8,128)(2,1)}), bf16[32,32,512]{2,1,0:T(8,128)(2,1)}, u32[]{:S(2)}, u32[]{:S(2)}) async-start(bf16[32,32,512]{2,1,0:T(8,128)(2,1)} %multiply_convert_fusion), calls=%async_computation.6 | async-start | bytes 2097152 | tf_op jit(solution)/shard_map/all_to_all | solution.py:153
  599.8 43.9 %all-gather.2.cloned.1.call-start = ((), (), s32[]{:S(2)}) async-start(), calls=%async_computation.7 | async-start | bytes 2359296 | tf_op jit(solution)/shard_map/all_gather | solution.py:164
  600.1 6.0 copy-start.6
  615.8 32.8 %copy-start.3 = (f32[1024,512]{1,0:T(8,128)}, f32[1024,512]{1,0:T(8,128)S(1)}, u32[]{:S(2)}) copy-start(f32[1024,512]{1,0:T(8,128)S(1)} %reshape.234) | copy-start | bytes 6291460
  643.7 2.6 copy-start.15
  644.9 1.3 copy-start.2
  648.5 38.6 %all-to-all-start.5 = ((bf16[32,32,512]{2,1,0:T(8,128)(2,1)}), bf16[32,32,512]{2,1,0:T(8,128)(2,1)S(1)}, u32[]{:S(2)}, u32[]{:S(2)}) async-start(bf16[32,32,512]{2,1,0:T(8,128)(2,1)} %bitcast.12), calls=%async_computation.5 | async-start | bytes 2097152 | tf_op jit(solution)/shard_map/all_to_all | solution.py:170
Sparse Core Ops, SparseCore 0:
  612.7 30.9 all-gather.1
